TPU v7x, 32 devices: a whole 2x2x4 slice. The times are simulated.
32 devices in a mesh: panel: 4 (over y, x), cap: 4 (over z), obs: 2 (over core).
Axes of the slice: x: 2, y: 2, z: 4, core: 2. Of those that a mesh axis runs over, the one named last changes fastest.
Arguments:
- surface: bfloat16 [2, 8192, 2560], P(None, ('panel', 'cap', 'obs')), may hold values from -6 to 6
- cap_of: int32 [8192], P(('panel', 'cap', 'obs')), may hold values from 0 to 31
- shift: int32 [64, 4], P(('panel', 'cap')), may hold values from 0 to 4
- amplitude: bfloat16 [3, 8192, 512], P(None, ('panel', 'cap'), 'obs'), may hold values from -0.09375 to 0.09375
Outputs:
- spectra: float32 [2, 256, 256], P('obs', ('panel', 'cap'))
Inputs may be any that keep to these rules, and one draw needn't show every extreme that they name: `cap_of`: a panel with a value below 16 lies on that outflow cap; other panels lie on the lateral surface.
All inputs are finite; a program needn't handle non-finite values.
Results may differ from a plain program's by a relative error of at most 0.0011.
Values may be sent and summed in bfloat16 or wider, within the bound.
A program may use at most 64 MiB of HBM per device.

v0:
```python
import jax
import jax.numpy as jnp
from jax import lax
from jax.sharding import PartitionSpec as P

BLK = 128
KMAX = 4
CAPS = 16
SEG = 512
NSEG = 7
HOP = 256
NBIN = 256
NT = 2048


def make_series(surface, cap_of):
    weight = jnp.where(cap_of >= CAPS, jnp.float32(1.0), jnp.float32(1.0 / CAPS))
    values = surface.astype(jnp.float32)
    after = jnp.concatenate([values[:, :, 1:], values[:, :, -1:]], axis=2)
    before = jnp.concatenate([values[:, :, :1], values[:, :, :-1]], axis=2)
    rates = (after - before) * 0.5
    stacked = jnp.stack([rates[0], rates[1], values[1]], axis=0) * weight[None, :, None]
    return stacked.astype(jnp.bfloat16)


def partial_signal(whole, amp, delays, base, length):
    terms, panels, samples = whole.shape
    ptiles = panels // BLK
    columns = amp.shape[2]
    otiles = columns // BLK
    tiles = whole.reshape(terms, ptiles, BLK, samples).transpose(1, 0, 2, 3)
    blocks = amp.reshape(terms, ptiles, BLK, otiles, BLK).transpose(1, 0, 2, 3, 4)

    def step(total, inputs):
        tile, delay_row, block = inputs
        windows = jax.vmap(
            lambda k: lax.dynamic_slice_in_dim(tile, base + (KMAX - k) * BLK, length, 2)
        )(delay_row)
        return (
            total
            + jnp.einsum("cbqo,qcbn->qon", block, windows, preferred_element_type=jnp.float32),
            None,
        )

    start = jnp.zeros((otiles, BLK, length), jnp.float32)
    total = lax.scan(step, start, (tiles, delays, blocks))[0]
    return total.reshape(columns, length)


def reduce_rows(partial_value):
    return lax.psum_scatter(partial_value, ("panel", "cap"), scatter_dimension=1, tiled=True)


def welch(signal):
    steps_n = jnp.arange(SEG, dtype=jnp.float32)
    hann = 0.5 - 0.5 * jnp.cos(2.0 * jnp.pi * steps_n / SEG)
    pieces = jnp.stack([signal[:, j * HOP : j * HOP + SEG] for j in range(NSEG)], axis=1) * hann
    index_n = jnp.arange(SEG, dtype=jnp.int32)
    index_f = jnp.arange(NBIN, dtype=jnp.int32)
    phase = (index_n[:, None] * index_f[None, :] % SEG).astype(jnp.float32) * (2.0 * jnp.pi / SEG)
    table = jnp.concatenate([jnp.cos(phase), -jnp.sin(phase)], axis=1)
    rows = signal.shape[0]
    spectrum = jnp.dot(
        pieces.reshape(rows * NSEG, SEG),
        table,
        precision=lax.Precision.HIGHEST,
        preferred_element_type=jnp.float32,
    )
    real_part = spectrum[:, :NBIN]
    imag_part = spectrum[:, NBIN:]
    power = (real_part * real_part + imag_part * imag_part).reshape(rows, NSEG, NBIN)
    return jnp.mean(power, axis=1) / jnp.sum(hann * hann)


def shards(surface, cap_of, shift, amplitude):
    local_series = make_series(surface, cap_of)
    whole = lax.all_gather(local_series, "obs", axis=1, tiled=True)
    otiles = amplitude.shape[2] // BLK
    delays = lax.dynamic_slice_in_dim(shift, lax.axis_index("obs") * otiles, otiles, 1)
    signal = partial_signal(whole, amplitude, delays, 0, NT)
    series_obs = reduce_rows(signal[None])[0]
    return welch(series_obs)[None]


def solution(mesh):
    return jax.shard_map(
        shards,
        mesh=mesh,
        in_specs=(
            P(None, ("panel", "cap", "obs"), None),
            P(("panel", "cap", "obs")),
            P(("panel", "cap"), None),
            P(None, ("panel", "cap"), "obs"),
        ),
        out_specs=P("obs", ("panel", "cap"), None),
        check_vma=False,
    )
```

profile of v0, /device:TPU:0, one launch (start us, length us, event | category | flops | bytes accessed | tf_op | source)
XLA Modules:
  0.0 186.7 jit_solution(11496227462698726981)
XLA Ops:
  6.5 4.5 %fusion.22 = (f32[2,256,2559]{2,1,0:T(8,128)S(1)}, f32[2,256,2559]{2,1,0:T(8,128)S(1)}) fusion(bf16[2,256,2560]{2,1,0:T(8,128)(2,1)} %param.6), kind=kLoop, calls=%fused_computation.48 | loop fusion | bytes 20963328 | tf_op jit(solution)/shard_map/slice | solution.py:20
  11.2 0.3 slice.78
  11.5 0.3 copy-done.3
  11.8 2.2 %fusion.5 = f32[2,256,2560]{2,1,0:T(8,128)S(1)} fusion(f32[2,256,1]{2,1,0:T(8,128)S(1)} %get-tuple-element.92, f32[2,256,2559]{2,1,0:T(8,128)S(1)} %get-tuple-element.94, f32[2,256,2559]{2,1,0:T(8,128)S(1)} %get-tuple-element.93, f32[2,256,1]{2,1,0:T(8,128)S(1)} %get-tuple-element.91), kind=kLoop, calls=%fused_computation.14 | loop fusion | flops 5242880 | bytes 15728640 | tf_op jit(solution)/shard_map/mul | solution.py:21
  14.0 3.1 %fusion.4 = bf16[3,256,2560]{2,1,0:T(8,128)(2,1)} fusion(f32[1,256,2560]{2,1,0:T(8,128)S(1)} %slice.78, f32[2,256,2560]{2,1,0:T(8,128)S(1)} %fusion.5, f32[256]{0:T(256)S(1)} %compare_select_fusion.1), kind=kLoop, calls=%fused_computation.12 | loop fusion | flops 5898240 | bytes 11797504 | tf_op jit(solution)/shard_map/convert_element_type | solution.py:23
  17.1 1.0 copy-done.2
  18.2 0.2 reshape.59
  18.5 20.6 %all-gather.2.cloned.1.call-done = bf16[3,512,2560]{2,1,0:T(8,128)(2,1)} async-done(((bf16[3,256,2560]{2,1,0:T(8,128)(2,1)}), bf16[3,512,2560]{2,1,0:T(8,128)(2,1)}) %all-gather.2.cloned.1.call-update) | async-done | bytes 7864336 | tf_op jit(solution)/shard_map/all_gather | solution.py:77
  39.0 51.4 %while.15 = (s32[]{:T(128)}, f32[2,128,2048]{2,1,0:T(8,128)}, bf16[4,3,128,2,128]{4,3,2,0,1:T(2,128)(2,1)S(1)}, bf16[4,3,128,2560]{3,2,0,1:T(8,128)(2,1)}, s32[4...) while((s32[]{:T(128)}, f32[2,128,2048]{2,1,0:T(8,128)}, ...), condition=%wide.region_1.2_spmd.clone, body=%wide.region_0.1_spmd.clone.sunk | while | flops 403701760 | bytes 15402304 | solution.py:46
  39.0 1.7 dynamic-slice_bitcast_fusion.2
  40.9 6.1 %while.16 = (s32[]{:T(128)}, bf16[3,128,2560]{2,1,0:T(8,128)(2,1)S(1)}, s32[2,3]{1,0:T(2,128)S(1)}, bf16[2,3,128,2048]{3,2,1,0:T(8,128)(2,1)}, s32[]{:T(128)}) while((s32[]{:T(128)}, bf16[3,128,2560]{2,1,0:T(8,128)(2,1)S(1)}, s32[2,3]{1,0:T(2,128)S(1)}, bf16[2,3,128,2048]{3,2,1,0:T(8,128)(2,1)}, s32[]{:T(128)}) %tuple.50), condition=%wide.while_cond, body=%wide.while_body.sunk | while | flops 2 | bytes 3146849 | solution.py:37
  40.9 0.6 slice.106
  41.5 2.5 %bitcast_dynamic-update-slice_fusion.2 = bf16[2,3,128,2048]{3,2,1,0:T(8,128)(2,1)} fusion(bf16[2,3,128,2048]{3,2,1,0:T(8,128)(2,1)} %get-tuple-element.179, s32[]{:T(128)} %get-tuple-element.176, bf16[3,128,2560]{2,1,0:T(8,128)(2,1)S(1)} %get-tuple-element.182, s32[]{:T(128)} %bitcast.51), kind=kLoop, calls=%fused_computation.clone.1 | loop fusion | bytes 3146752 | tf_op jit(solution)/shard_map/while/body/eval_jaxpr/vmap()/gather
  44.0 0.6 slice.106
  44.6 2.4 %bitcast_dynamic-update-slice_fusion.2 = bf16[2,3,128,2048]{3,2,1,0:T(8,128)(2,1)} fusion(bf16[2,3,128,2048]{3,2,1,0:T(8,128)(2,1)} %get-tuple-element.179, s32[]{:T(128)} %get-tuple-element.176, bf16[3,128,2560]{2,1,0:T(8,128)(2,1)S(1)} %get-tuple-element.182, s32[]{:T(128)} %bitcast.51), kind=kLoop, calls=%fused_computation.clone.1 | loop fusion | bytes 3146752 | tf_op jit(solution)/shard_map/while/body/eval_jaxpr/vmap()/gather
  47.1 0.2 copy.22
  47.3 4.1 %fusion.30 = f32[2,128,2048]{2,1,0:T(8,128)} fusion(bf16[2,3,128,2048]{3,2,1,0:T(8,128)(2,1)} %get-tuple-element.165, f32[2,128,2048]{2,1,0:T(8,128)} %get-tuple-element.195, pred[]{:T(512)S(6)} %compare.7, bf16[1,3,128,2,128]{2,4,1,3,0:T(8,128)(2,1)S(1)} %copy.22), kind=kOutput, calls=%fused_computation.3.clone.1 | convolution fusion | flops 403701760 | bytes 7536641 | tf_op jit(solution)/shard_map/while/body/eval_jaxpr/cbqo,qcbn->qon/dot_general | solution.py:41
  51.4 1.7 dynamic-slice_bitcast_fusion.2
  53.2 6.1 %while.16 = (s32[]{:T(128)}, bf16[3,128,2560]{2,1,0:T(8,128)(2,1)S(1)}, s32[2,3]{1,0:T(2,128)S(1)}, bf16[2,3,128,2048]{3,2,1,0:T(8,128)(2,1)}, s32[]{:T(128)}) while((s32[]{:T(128)}, bf16[3,128,2560]{2,1,0:T(8,128)(2,1)S(1)}, s32[2,3]{1,0:T(2,128)S(1)}, bf16[2,3,128,2048]{3,2,1,0:T(8,128)(2,1)}, s32[]{:T(128)}) %tuple.50), condition=%wide.while_cond, body=%wide.while_body.sunk | while | flops 2 | bytes 3146849 | solution.py:37
  53.3 0.6 slice.106
  53.9 2.5 %bitcast_dynamic-update-slice_fusion.2 = bf16[2,3,128,2048]{3,2,1,0:T(8,128)(2,1)} fusion(bf16[2,3,128,2048]{3,2,1,0:T(8,128)(2,1)} %get-tuple-element.179, s32[]{:T(128)} %get-tuple-element.176, bf16[3,128,2560]{2,1,0:T(8,128)(2,1)S(1)} %get-tuple-element.182, s32[]{:T(128)} %bitcast.51), kind=kLoop, calls=%fused_computation.clone.1 | loop fusion | bytes 3146752 | tf_op jit(solution)/shard_map/while/body/eval_jaxpr/vmap()/gather
  56.3 0.6 slice.106
  57.0 2.4 %bitcast_dynamic-update-slice_fusion.2 = bf16[2,3,128,2048]{3,2,1,0:T(8,128)(2,1)} fusion(bf16[2,3,128,2048]{3,2,1,0:T(8,128)(2,1)} %get-tuple-element.179, s32[]{:T(128)} %get-tuple-element.176, bf16[3,128,2560]{2,1,0:T(8,128)(2,1)S(1)} %get-tuple-element.182, s32[]{:T(128)} %bitcast.51), kind=kLoop, calls=%fused_computation.clone.1 | loop fusion | bytes 3146752 | tf_op jit(solution)/shard_map/while/body/eval_jaxpr/vmap()/gather
  59.5 0.2 copy.22
  59.7 4.7 %fusion.30 = f32[2,128,2048]{2,1,0:T(8,128)} fusion(bf16[2,3,128,2048]{3,2,1,0:T(8,128)(2,1)} %get-tuple-element.165, f32[2,128,2048]{2,1,0:T(8,128)} %get-tuple-element.195, pred[]{:T(512)S(6)} %compare.7, bf16[1,3,128,2,128]{2,4,1,3,0:T(8,128)(2,1)S(1)} %copy.22), kind=kOutput, calls=%fused_computation.3.clone.1 | convolution fusion | flops 403701760 | bytes 7536641 | tf_op jit(solution)/shard_map/while/body/eval_jaxpr/cbqo,qcbn->qon/dot_general | solution.py:41
  64.4 1.7 dynamic-slice_bitcast_fusion.2
  66.3 6.1 %while.16 = (s32[]{:T(128)}, bf16[3,128,2560]{2,1,0:T(8,128)(2,1)S(1)}, s32[2,3]{1,0:T(2,128)S(1)}, bf16[2,3,128,2048]{3,2,1,0:T(8,128)(2,1)}, s32[]{:T(128)}) while((s32[]{:T(128)}, bf16[3,128,2560]{2,1,0:T(8,128)(2,1)S(1)}, s32[2,3]{1,0:T(2,128)S(1)}, bf16[2,3,128,2048]{3,2,1,0:T(8,128)(2,1)}, s32[]{:T(128)}) %tuple.50), condition=%wide.while_cond, body=%wide.while_body.sunk | while | flops 2 | bytes 3146849 | solution.py:37
  66.3 0.6 slice.106
  66.9 2.5 %bitcast_dynamic-update-slice_fusion.2 = bf16[2,3,128,2048]{3,2,1,0:T(8,128)(2,1)} fusion(bf16[2,3,128,2048]{3,2,1,0:T(8,128)(2,1)} %get-tuple-element.179, s32[]{:T(128)} %get-tuple-element.176, bf16[3,128,2560]{2,1,0:T(8,128)(2,1)S(1)} %get-tuple-element.182, s32[]{:T(128)} %bitcast.51), kind=kLoop, calls=%fused_computation.clone.1 | loop fusion | bytes 3146752 | tf_op jit(solution)/shard_map/while/body/eval_jaxpr/vmap()/gather
  69.4 0.6 slice.106
  70.0 2.4 %bitcast_dynamic-update-slice_fusion.2 = bf16[2,3,128,2048]{3,2,1,0:T(8,128)(2,1)} fusion(bf16[2,3,128,2048]{3,2,1,0:T(8,128)(2,1)} %get-tuple-element.179, s32[]{:T(128)} %get-tuple-element.176, bf16[3,128,2560]{2,1,0:T(8,128)(2,1)S(1)} %get-tuple-element.182, s32[]{:T(128)} %bitcast.51), kind=kLoop, calls=%fused_computation.clone.1 | loop fusion | bytes 3146752 | tf_op jit(solution)/shard_map/while/body/eval_jaxpr/vmap()/gather
  72.5 0.2 copy.22
  72.7 4.7 %fusion.30 = f32[2,128,2048]{2,1,0:T(8,128)} fusion(bf16[2,3,128,2048]{3,2,1,0:T(8,128)(2,1)} %get-tuple-element.165, f32[2,128,2048]{2,1,0:T(8,128)} %get-tuple-element.195, pred[]{:T(512)S(6)} %compare.7, bf16[1,3,128,2,128]{2,4,1,3,0:T(8,128)(2,1)S(1)} %copy.22), kind=kOutput, calls=%fused_computation.3.clone.1 | convolution fusion | flops 403701760 | bytes 7536641 | tf_op jit(solution)/shard_map/while/body/eval_jaxpr/cbqo,qcbn->qon/dot_general | solution.py:41
  77.4 1.7 dynamic-slice_bitcast_fusion.2
  79.3 6.1 %while.16 = (s32[]{:T(128)}, bf16[3,128,2560]{2,1,0:T(8,128)(2,1)S(1)}, s32[2,3]{1,0:T(2,128)S(1)}, bf16[2,3,128,2048]{3,2,1,0:T(8,128)(2,1)}, s32[]{:T(128)}) while((s32[]{:T(128)}, bf16[3,128,2560]{2,1,0:T(8,128)(2,1)S(1)}, s32[2,3]{1,0:T(2,128)S(1)}, bf16[2,3,128,2048]{3,2,1,0:T(8,128)(2,1)}, s32[]{:T(128)}) %tuple.50), condition=%wide.while_cond, body=%wide.while_body.sunk | while | flops 2 | bytes 3146849 | solution.py:37
  79.3 0.6 slice.106
  79.9 2.5 %bitcast_dynamic-update-slice_fusion.2 = bf16[2,3,128,2048]{3,2,1,0:T(8,128)(2,1)} fusion(bf16[2,3,128,2048]{3,2,1,0:T(8,128)(2,1)} %get-tuple-element.179, s32[]{:T(128)} %get-tuple-element.176, bf16[3,128,2560]{2,1,0:T(8,128)(2,1)S(1)} %get-tuple-element.182, s32[]{:T(128)} %bitcast.51), kind=kLoop, calls=%fused_computation.clone.1 | loop fusion | bytes 3146752 | tf_op jit(solution)/shard_map/while/body/eval_jaxpr/vmap()/gather
  82.4 0.6 slice.106
  83.0 2.4 %bitcast_dynamic-update-slice_fusion.2 = bf16[2,3,128,2048]{3,2,1,0:T(8,128)(2,1)} fusion(bf16[2,3,128,2048]{3,2,1,0:T(8,128)(2,1)} %get-tuple-element.179, s32[]{:T(128)} %get-tuple-element.176, bf16[3,128,2560]{2,1,0:T(8,128)(2,1)S(1)} %get-tuple-element.182, s32[]{:T(128)} %bitcast.51), kind=kLoop, calls=%fused_computation.clone.1 | loop fusion | bytes 3146752 | tf_op jit(solution)/shard_map/while/body/eval_jaxpr/vmap()/gather
  85.5 0.2 copy.22
  85.7 4.7 %fusion.30 = f32[2,128,2048]{2,1,0:T(8,128)} fusion(bf16[2,3,128,2048]{3,2,1,0:T(8,128)(2,1)} %get-tuple-element.165, f32[2,128,2048]{2,1,0:T(8,128)} %get-tuple-element.195, pred[]{:T(512)S(6)} %compare.7, bf16[1,3,128,2,128]{2,4,1,3,0:T(8,128)(2,1)S(1)} %copy.22), kind=kOutput, calls=%fused_computation.3.clone.1 | convolution fusion | flops 403701760 | bytes 7536641 | tf_op jit(solution)/shard_map/while/body/eval_jaxpr/cbqo,qcbn->qon/dot_general | solution.py:41
  90.5 0.7 multiply_reduce_fusion
  91.2 2.1 %sine_negate_fusion = (f32[512,256]{1,0:T(8,128)S(1)}, f32[512,256]{1,0:T(8,128)S(1)}) fusion(), kind=kLoop, calls=%fused_computation.25 | loop fusion | flops 1966080 | bytes 1048576 | tf_op jit(solution)/shard_map/neg | solution.py:61
  93.3 82.9 %reduce-scatter.2.cloned.1.call-done = f32[1,16,2048]{2,1,0:T(8,128)} async-done(((f32[1,256,2048]{2,1,0:T(8,128)}), f32[1,16,2048]{2,1,0:T(8,128)}) %reduce-scatter.2.cloned.1.call-update) | async-done | bytes 131088 | tf_op jit(solution)/shard_map/reduce_scatter | solution.py:51
  176.2 0.9 fusion.23
  177.4 0.3 stack.38
  177.8 0.7 fusion.6
  178.6 1.2 divide_bitcast_fusion
  (54 shorter events, 2.0 us)
Async XLA Ops:
  6.5 11.8 %copy-start = (s32[4,4]{1,0:T(4,128)S(1)}, s32[4,4]{1,0:T(4,128)}, u32[]{:S(2)}) copy-start(s32[4,4]{1,0:T(4,128)} %param.8) | copy-start | bytes 196
  6.5 4.5 %copy-start.1 = (bf16[2,256,2560]{2,1,0:T(8,128)(2,1)S(1)}, bf16[2,256,2560]{2,1,0:T(8,128)(2,1)}, u32[]{:S(2)}) copy-start(bf16[2,256,2560]{2,1,0:T(8,128)(2,1)} %param.6) | copy-start | bytes 7864324
  6.5 32.5 %all-gather.2.cloned.1.call-start = ((), (), s32[]{:S(2)}) async-start(), calls=%async_computation.1 | async-start | bytes 11796480 | tf_op jit(solution)/shard_map/all_gather | solution.py:77
  11.1 0.7 copy-start.3
  17.1 1.1 copy-start.2
  17.1 159.2 %reduce-scatter.2.cloned.1.call-start = ((), (), s32[]{:S(2)}) async-start(), calls=%async_computation.2 | async-start | bytes 2228224 | tf_op jit(solution)/shard_map/reduce_scatter | solution.py:51
Sparse Core Ops, SparseCore 0:
  17.2 21.7 all-gather.1
  90.6 85.6 reduce-scatter.1
where the time goes:
time: 187 us
  waiting for transfers between devices  104 us (56%)
  local copies, waits for them, and re-layouts  41 us (22%)
  matrix products  19 us (10%)
  between operations  13.6 us (7%)
  other arithmetic  9.47 us (5%)
    reduce_scatter x1, waiting for transfers between devices, reduce_rows(): lax.psum_scatter(partial_value, ('panel', 'cap'), scatter_dimension=1, ti...  82.9 us
    gather x24, local copies, waits for them, and re-layouts  24.4 us
    all_gather x1, waiting for transfers between devices, shards(): whole = lax.all_gather(local_series, 'obs', axis=1, tiled=True)  20.6 us
    dot_general x4, matrix products, step(): jnp.einsum('cbqo,qcbn->qon', block, windows, preferred_element_type=jnp.f...  18.3 us
    squeeze x4, local copies, waits for them, and re-layouts, partial_signal(): total = lax.scan(step, start, (tiles, delays, blocks))[0]  6.69 us
    slice x2, local copies, waits for them, and re-layouts, make_series(): before = jnp.concatenate([values[:, :, :1], values[:, :, :-1]], axis=2)  4.62 us
  transfers between devices with their start and end apart: 2, of which 2 were waited for; matrix products, arithmetic and copies ran while one was open for 2% of the time, Pallas kernels for 0%

commit v1 on v0

--- a/solution.py
+++ b/solution.py
@@ -1,6 +1,11 @@
+import functools
+
 import jax
 import jax.numpy as jnp
+import numpy as np
 from jax import lax
+from jax.experimental import pallas as pl
+from jax.experimental.pallas import tpu as pltpu
 from jax.sharding import PartitionSpec as P
 
 BLK = 128
@@ -82,9 +87,250 @@
     return welch(series_obs)[None]
 
 
+MESH = pl.DeviceIdType.MESH
+FULL = 32000.0
+CHUNK = 512
+
+
+def dft_tables():
+    n = np.arange(SEG)
+    hann = 0.5 - 0.5 * np.cos(2.0 * np.pi * n / SEG)
+    phase = (n[:, None] * np.arange(NBIN)[None, :] % SEG) * (2.0 * np.pi / SEG)
+    table = np.concatenate([np.cos(phase), -np.sin(phase)], axis=1) * hann[:, None]
+    high = table.astype(jnp.bfloat16)
+    low = (table - high.astype(np.float64)).astype(jnp.bfloat16)
+    return high, low, float(np.sum(hann * hann)) * NSEG
+
+
+def scale_of(largest):
+    return jnp.exp2(jnp.ceil(jnp.log2(jnp.maximum(largest, 1e-30))))
+
+
+def biggest(values):
+    return jnp.max(jnp.abs(values), axis=(0, 1), keepdims=True)
+
+
+def code(values, scale):
+    return jnp.round(values * (FULL / scale)).astype(jnp.int32).astype(jnp.int16)
+
+
+def decode(coded, scale):
+    return coded.astype(jnp.float32) * (scale * (1.0 / FULL))
+
+
+def fused(
+    norm, shift_ref, surf_ref, cap_ref, amp_ref, high_ref, low_ref, out_ref,
+    series, lhs, acc, other, amp_in,
+    send_c, recv_c, send_a, recv_a, send_b, recv_b, send_z, recv_z,
+    scale_out, scale_in, sem_amp, sem_data, sem_scale,
+):
+    panel, cap, obs = lax.axis_index("panel"), lax.axis_index("cap"), lax.axis_index("obs")
+    y, x = panel // 2, panel % 2
+    to_core = {"obs": 1 - obs}
+    to_y = {"panel": (1 - y) * 2 + x}
+    to_x = {"panel": y * 2 + 1 - x}
+    caps = 4
+    to_z = [{"cap": lax.rem(cap + d, caps)} for d in range(1, caps)]
+
+    barrier = pltpu.get_barrier_semaphore()
+    for target in [to_core, to_y, to_x] + to_z:
+        pl.semaphore_signal(barrier, inc=1, device_id=target, device_id_type=MESH)
+    pl.semaphore_wait(barrier, 6)
+
+    def remote(src, dst, sems, number, target):
+        return pltpu.make_async_remote_copy(
+            src_ref=src, dst_ref=dst, send_sem=sems.at[0, number], recv_sem=sems.at[1, number],
+            device_id=target, device_id_type=MESH,
+        )
+
+    half = 2 * BLK
+    amp_copy = remote(amp_ref.at[:, pl.ds(pl.multiple_of((1 - obs) * half, half), half), :], amp_in, sem_amp, 0, to_core)
+    amp_copy.start()
+
+    weight = jnp.where(cap_ref[...] >= CAPS, 1.0, 1.0 / CAPS).astype(jnp.float32)
+    for tile in range(2):
+        rows = slice(tile * BLK, (tile + 1) * BLK)
+        for term in range(2):
+            v = surf_ref[term, rows, :]
+            after = jnp.concatenate([v[:, 1:], v[:, -1:]], axis=1)
+            before = jnp.concatenate([v[:, :1], v[:, :-1]], axis=1)
+            rate = after - before
+            for b in range(v.shape[1] // BLK):
+                series[tile, b, term * BLK:(term + 1) * BLK, :] = rate[:, b * BLK:(b + 1) * BLK]
+                if term == 1:
+                    series[tile, b, 2 * BLK:3 * BLK, :] = v[:, b * BLK:(b + 1) * BLK]
+
+    def fill(side, load):
+        for tile in range(2):
+            w = weight[:, tile * BLK:(tile + 1) * BLK]
+            for part in range(2):
+                for term in range(3):
+                    block = load(term, tile, part).astype(jnp.float32).T
+                    lhs[side * 2 + part, tile, :, term * BLK:(term + 1) * BLK] = (
+                        block * (w * (1.0 if term == 2 else 0.5))
+                    ).astype(jnp.bfloat16)
+
+    fill(0, lambda term, tile, part: amp_ref[
+        term, pl.ds(pl.multiple_of(obs * half + tile * BLK, BLK), BLK), part * BLK:(part + 1) * BLK])
+    amp_copy.wait()
+    fill(1, lambda term, tile, part: amp_in[term, tile * BLK:(tile + 1) * BLK, part * BLK:(part + 1) * BLK])
+
+    def product(side, part, target, base):
+        column = (obs if side == 0 else 1 - obs) * 2 + part
+        largest = jnp.zeros((1, 1), jnp.float32)
+        for i in range(NT // CHUNK):
+            total = jnp.zeros((BLK, CHUNK), jnp.float32)
+            for tile in range(2):
+                begin = KMAX - shift_ref[obs * 2 + tile, column] + i * (CHUNK // BLK)
+                window = jnp.concatenate([series[tile, begin + b] for b in range(CHUNK // BLK)], axis=1)
+                total += jnp.dot(
+                    lhs[side * 2 + part, tile], window,
+                    preferred_element_type=jnp.float32,
+                )
+            target[base:base + BLK, i * CHUNK:(i + 1) * CHUNK] = total
+            largest = jnp.maximum(largest, biggest(total))
+        return largest
+
+    pending = []
+
+    def send(number, scale, src, dst, target):
+        scale_out[number] = jnp.broadcast_to(scale, (8, 128))
+        for copy in (
+            remote(scale_out.at[number], scale_in.at[number], sem_scale, number, target),
+            remote(src, dst, sem_data, number, target),
+        ):
+            copy.start()
+            pending.append(copy)
+        return pending[-2:]
+
+    def take(number):
+        return scale_in[number][0:1, 0:1]
+
+    core_copies = []
+    for part in range(2):
+        scale = scale_of(product(1, part, other, 0))
+        send_c[part] = code(other[...], scale)
+        core_copies += send(part, scale, send_c.at[part], recv_c.at[part], to_core)
+    for part in range(2):
+        product(0, part, acc, part * BLK)
+    for part in range(2):
+        for copy in core_copies[2 * part:2 * part + 2]:
+            copy.wait_recv()
+        acc[part * BLK:(part + 1) * BLK, :] += decode(recv_c[part], take(part))
+
+    mid = NT // 2
+    quarter = BLK // 2
+    early, late = slice(0, mid), slice(mid, NT)
+
+    def at(row, size):
+        return pl.ds(pl.multiple_of(row, quarter), size)
+
+    give = acc[at((1 - y) * BLK, BLK), early]
+    scale = scale_of(biggest(give))
+    send_a[0] = code(give, scale)
+    a_early = send(2, scale, send_a.at[0], recv_a.at[0], to_y)
+    upper = acc[at((1 - x) * quarter, quarter), late]
+    lower = acc[at(BLK + (1 - x) * quarter, quarter), late]
+    scale = scale_of(jnp.maximum(biggest(upper), biggest(lower)))
+    send_a[1, 0:quarter] = code(upper, scale)
+    send_a[1, quarter:BLK] = code(lower, scale)
+    a_late = send(3, scale, send_a.at[1], recv_a.at[1], to_x)
+
+    for copy in a_early:
+        copy.wait_recv()
+    acc[at(y * BLK, BLK), early] += decode(recv_a[0], take(2))
+    give = acc[at(y * BLK + (1 - x) * quarter, quarter), early]
+    scale = scale_of(biggest(give))
+    send_b[0] = code(give, scale)
+    b_early = send(4, scale, send_b.at[0], recv_b.at[0], to_x)
+    for copy in a_late:
+        copy.wait_recv()
+    for part in range(2):
+        acc[at(part * BLK + x * quarter, quarter), late] += decode(
+            recv_a[1, part * quarter:(part + 1) * quarter], take(3))
+    give = acc[at((1 - y) * BLK + x * quarter, quarter), late]
+    scale = scale_of(biggest(give))
+    send_b[1] = code(give, scale)
+    b_late = send(5, scale, send_b.at[1], recv_b.at[1], to_y)
+
+    mine = at(y * BLK + x * quarter, quarter)
+    for number, columns, copies in ((0, early, b_early), (1, late, b_late)):
+        for copy in copies:
+            copy.wait_recv()
+        acc[mine, columns] += decode(recv_b[number], take(4 + number))
+
+    rows = quarter // caps
+    whole = acc[mine, :]
+    scale = scale_of(biggest(whole))
+    send_z[...] = code(whole, scale)
+    z_copies = []
+    for d in range(1, caps):
+        place = pl.multiple_of(lax.rem(cap + d, caps) * rows, rows)
+        z_copies.append(send(5 + d, scale, send_z.at[pl.ds(place, rows)], recv_z.at[d - 1], to_z[d - 1]))
+    signal = acc[pl.ds(pl.multiple_of(y * BLK + x * quarter + cap * rows, rows), rows), :]
+    for d in range(1, caps):
+        for copy in z_copies[d - 1]:
+            copy.wait_recv()
+        signal += decode(recv_z[d - 1], take(5 + d))
+
+    pieces = jnp.concatenate([signal[:, j * HOP:j * HOP + SEG] for j in range(NSEG)], axis=0)
+    top = pieces.astype(jnp.bfloat16)
+    rest = (pieces - top.astype(jnp.float32)).astype(jnp.bfloat16)
+    dot = functools.partial(jnp.dot, preferred_element_type=jnp.float32)
+    spectrum = dot(top, high_ref[...]) + (dot(rest, high_ref[...]) + dot(top, low_ref[...]))
+    power = spectrum[:, :NBIN] ** 2 + spectrum[:, NBIN:] ** 2
+    total = power[0:rows]
+    for j in range(1, NSEG):
+        total += power[j * rows:(j + 1) * rows]
+    out_ref[...] = total * (1.0 / norm)
+
+    for copy in pending:
+        copy.wait_send()
+
+
+def fused_shards(surface, cap_of, shift, amplitude):
+    high, low, norm = dft_tables()
+    vmem = pl.BlockSpec(memory_space=pltpu.VMEM)
+    rows = BLK // 8
+    out = pl.pallas_call(
+        functools.partial(fused, norm),
+        out_shape=jax.ShapeDtypeStruct((rows, NBIN), jnp.float32),
+        in_specs=[pl.BlockSpec(memory_space=pltpu.SMEM)] + [vmem] * 5,
+        out_specs=vmem,
+        scratch_shapes=[
+            pltpu.VMEM((2, surface.shape[2] // BLK, 3 * BLK, BLK), jnp.bfloat16),
+            pltpu.VMEM((4, 2, BLK, 3 * BLK), jnp.bfloat16),
+            pltpu.VMEM((2 * BLK, NT), jnp.float32),
+            pltpu.VMEM((BLK, NT), jnp.float32),
+            pltpu.VMEM((3, 2 * BLK, 2 * BLK), jnp.bfloat16),
+            pltpu.VMEM((2, BLK, NT), jnp.int16),
+            pltpu.VMEM((2, BLK, NT), jnp.int16),
+            pltpu.VMEM((2, BLK, NT // 2), jnp.int16),
+            pltpu.VMEM((2, BLK, NT // 2), jnp.int16),
+            pltpu.VMEM((2, BLK // 2, NT // 2), jnp.int16),
+            pltpu.VMEM((2, BLK // 2, NT // 2), jnp.int16),
+            pltpu.VMEM((BLK // 2, NT), jnp.int16),
+            pltpu.VMEM((3, rows, NT), jnp.int16),
+            pltpu.VMEM((9, 8, 128), jnp.float32),
+            pltpu.VMEM((9, 8, 128), jnp.float32),
+            pltpu.SemaphoreType.DMA((2, 1)),
+            pltpu.SemaphoreType.DMA((2, 9)),
+            pltpu.SemaphoreType.DMA((2, 9)),
+        ],
+        compiler_params=pltpu.CompilerParams(
+            collective_id=0, has_side_effects=True, vmem_limit_bytes=48 * 1024 * 1024
+        ),
+    )(shift, surface, cap_of.reshape(1, -1), amplitude, jnp.asarray(high), jnp.asarray(low))
+    return out[None]
+
+
+def suits(mesh):
+    return mesh.shape["panel"] == 4 and mesh.shape["cap"] == 4 and mesh.shape["obs"] == 2
+
+
 def solution(mesh):
     return jax.shard_map(
-        shards,
+        fused_shards if suits(mesh) else shards,
         mesh=mesh,
         in_specs=(
             P(None, ("panel", "cap", "obs"), None),

time: 187 us -> 39.2 us (0.21)
  waiting for transfers between devices: 104 us -> 0 us
  local copies, waits for them, and re-layouts: 41 us -> 6.92 us
  Pallas kernels: 0 us -> 31.9 us
  matrix products: 19 us -> 0 us
  between operations: 13.6 us -> 0.02 us
  other arithmetic: 9.47 us -> 0 us
    reduce_scatter x1 -> x0, waiting for transfers between devices: 82.9 us -> none  [reduce_rows(): lax.psum_scatter(partial_value, ('panel', 'cap'), scatter_dimension=1, ti...]
    pallas_call x0 -> x1, Pallas kernels: none -> 31.9 us  [fused_shards(): pl.pallas_call(functools.partial(fused, norm), out_shape=jax.ShapeDtypeSt...]
    gather x24 -> x0, local copies, waits for them, and re-layouts: 24.4 us -> none
    all_gather x1 -> x0, waiting for transfers between devices: 20.6 us -> none  [shards(): whole = lax.all_gather(local_series, 'obs', axis=1, tiled=True)]
    dot_general x5 -> x0, matrix products: 19 us -> none  [the longest x4 18.3 us: step(): jnp.einsum('cbqo,qcbn->qon', block, windows, preferred_element_type=jnp.f...]
    squeeze x4 -> x0, local copies, waits for them, and re-layouts: 6.69 us -> none  [partial_signal(): total = lax.scan(step, start, (tiles, delays, blocks))[0]]
    slice x4 -> x0, local copies, waits for them, and re-layouts: 5.79 us -> none  [the longest x2 4.62 us: make_series(): before = jnp.concatenate([values[:, :, :1], values[:, :, :-1]], axis=2)]
    unnamed x8 -> x13, local copies, waits for them, and re-layouts: 1.31 us -> 6.92 us
  transfers between devices with their start and end apart: 2 -> 0, of which waited for: 2 -> 0; matrix products, arithmetic and copies ran while one was open for 2% -> 0% of each run, Pallas kernels for 0% -> 0%
where the time goes in v1:
time: 39.2 us; the launch traced here: 38.9 us
  Pallas kernels  31.9 us (81%)
  local copies, waits for them, and re-layouts  6.92 us (18%)
    pallas_call x1, Pallas kernels, fused_shards(): pl.pallas_call(functools.partial(fused, norm), out_shape=jax.ShapeDtypeSt...  31.9 us
    unnamed x13, local copies, waits for them, and re-layouts  6.92 us

profile of v1, /device:TPU:0, one launch (start us, length us, event | category | flops | bytes accessed | tf_op | source)
XLA Modules:
  0.0 38.9 jit_solution(1769842236276640972)
XLA Ops:
  0.0 0.0 copy-start
  0.0 1.7 %copy-done = bf16[2,256,2560]{2,1,0:T(8,128)(2,1)S(1)} copy-done((bf16[2,256,2560]{2,1,0:T(8,128)(2,1)S(1)}, bf16[2,256,2560]{2,1,0:T(8,128)(2,1)}, u32[]{:S(2)}) %copy-start) | copy-done | bytes 2621464
  1.7 0.0 copy-start.1
  1.7 1.1 %copy-done.1 = bf16[3,512,256]{2,1,0:T(8,128)(2,1)S(1)} copy-done((bf16[3,512,256]{2,1,0:T(8,128)(2,1)S(1)}, bf16[3,512,256]{2,1,0:T(8,128)(2,1)}, u32[]{:S(2)}) %copy-start.1) | copy-done | bytes 786456
  2.9 0.0 copy-start.2
  2.9 1.0 %copy-done.2 = bf16[512,512]{1,0:T(8,128)(2,1)S(1)} copy-done((bf16[512,512]{1,0:T(8,128)(2,1)S(1)}, bf16[512,512]{1,0:T(8,128)(2,1)}, u32[]{:S(2)}) %copy-start.2) | copy-done | bytes 524312
  3.9 0.0 copy-start.3
  3.9 1.0 %copy-done.3 = bf16[512,512]{1,0:T(8,128)(2,1)S(1)} copy-done((bf16[512,512]{1,0:T(8,128)(2,1)S(1)}, bf16[512,512]{1,0:T(8,128)(2,1)}, u32[]{:S(2)}) %copy-start.3) | copy-done | bytes 524312
  5.0 0.0 copy-start.4
  5.0 0.7 %copy-done.4 = s32[4,4]{1,0:T(4,128)S(1)} copy-done((s32[4,4]{1,0:T(4,128)S(1)}, s32[4,4]{1,0:T(4,128)}, u32[]{:S(2)}) %copy-start.4) | copy-done | bytes 88
  5.6 0.0 copy-start.5
  5.6 0.7 %copy-done.5 = s32[256]{0:T(256)S(1)} copy-done((s32[256]{0:T(256)S(1)}, s32[256]{0:T(256)}, u32[]{:S(2)}) %copy-start.5) | copy-done | bytes 1048
  6.3 31.9 %shard_map.64 = f32[16,256]{1,0:T(8,128)S(1)} custom-call(s32[4,4]{1,0:T(4,128)S(1)} %copy-done.4, bf16[2,256,2560]{2,1,0:T(8,128)(2,1)S(1)} %copy-done, s32[1,256]{1,0:T(1,128)S(1)} %bitcast.3, bf16[3,512,256]{2,1,0:T(8,128)(2,1)S(1)} %copy-done.1, bf16[512,512]{1,0:T(8,128)(2,1)S(1)} %copy-done.3, bf16[512,512]{1,0:T(8,128)(2,1)S(1)} %copy-done.2), custom_call_target="tpu_custom_call" | custom-call | tf_op jit(solution)/shard_map/pallas_call | solution.py:295
  38.3 0.6 %copy.8 = f32[1,16,256]{2,1,0:T(8,128)} copy(f32[1,16,256]{2,1,0:T(8,128)S(1)} %bitcast.2) | data formatting | bytes 32768
Async XLA Ops:
  0.0 1.7 %copy-start = (bf16[2,256,2560]{2,1,0:T(8,128)(2,1)S(1)}, bf16[2,256,2560]{2,1,0:T(8,128)(2,1)}, u32[]{:S(2)}) copy-start(bf16[2,256,2560]{2,1,0:T(8,128)(2,1)} %surf_ref.1) | copy-start | bytes 7864324
  1.7 1.1 %copy-start.1 = (bf16[3,512,256]{2,1,0:T(8,128)(2,1)S(1)}, bf16[3,512,256]{2,1,0:T(8,128)(2,1)}, u32[]{:S(2)}) copy-start(bf16[3,512,256]{2,1,0:T(8,128)(2,1)} %amp_ref.1) | copy-start | bytes 2359300
  2.9 1.0 %copy-start.2 = (bf16[512,512]{1,0:T(8,128)(2,1)S(1)}, bf16[512,512]{1,0:T(8,128)(2,1)}, u32[]{:S(2)}) copy-start(bf16[512,512]{1,0:T(8,128)(2,1)} %constant.5.clone.low_ref) | copy-start | bytes 1572868
  3.9 1.0 %copy-start.3 = (bf16[512,512]{1,0:T(8,128)(2,1)S(1)}, bf16[512,512]{1,0:T(8,128)(2,1)}, u32[]{:S(2)}) copy-start(bf16[512,512]{1,0:T(8,128)(2,1)} %constant.4.clone.high_ref) | copy-start | bytes 1572868
  5.0 0.7 %copy-start.4 = (s32[4,4]{1,0:T(4,128)S(1)}, s32[4,4]{1,0:T(4,128)}, u32[]{:S(2)}) copy-start(s32[4,4]{1,0:T(4,128)} %shift_ref.1) | copy-start | bytes 196
  5.6 0.7 %copy-start.5 = (s32[256]{0:T(256)S(1)}, s32[256]{0:T(256)}, u32[]{:S(2)}) copy-start(s32[256]{0:T(256)} %param.7) | copy-start | bytes 3076

commit v2 on v0

--- a/solution.py
+++ b/solution.py
@@ -1,6 +1,11 @@
+import functools
+
 import jax
 import jax.numpy as jnp
+import numpy as np
 from jax import lax
+from jax.experimental import pallas as pl
+from jax.experimental.pallas import tpu as pltpu
 from jax.sharding import PartitionSpec as P
 
 BLK = 128
@@ -82,9 +87,288 @@
     return welch(series_obs)[None]
 
 
+MESH = pl.DeviceIdType.MESH
+FULL = 32000.0
+CHUNK = 512
+CHIPS_Z = 4
+
+
+def dft_tables():
+    n = np.arange(SEG)
+    hann = 0.5 - 0.5 * np.cos(2.0 * np.pi * n / SEG)
+    phase = (n[:, None] * np.arange(NBIN)[None, :] % SEG) * (2.0 * np.pi / SEG)
+    table = np.concatenate([np.cos(phase), -np.sin(phase)], axis=1) * hann[:, None]
+    high = table.astype(jnp.bfloat16)
+    low = (table - high.astype(np.float64)).astype(jnp.bfloat16)
+    return high, low, float(np.sum(hann * hann)) * NSEG
+
+
+def scale_of(largest):
+    return jnp.exp2(jnp.ceil(jnp.log2(jnp.maximum(largest, 1e-30))))
+
+
+def biggest(values):
+    return jnp.max(jnp.abs(values), axis=(0, 1), keepdims=True)
+
+
+def code(values, scale):
+    return jnp.round(values * (FULL / scale)).astype(jnp.int32).astype(jnp.int16)
+
+
+def decode(coded, scale):
+    return coded.astype(jnp.float32) * (scale * (1.0 / FULL))
+
+
+def fused(
+    norm, shift_hbm, surf_hbm, cap_hbm, amp_hbm, high_hbm, low_hbm, out_ref,
+    shift_ref, surf_ref, cap_ref, amp_own, high_ref, low_ref, amp_in,
+    series, lhs, acc, other,
+    send_c, recv_c, send_a, recv_a, send_b, recv_b, send_z, recv_z,
+    scale_out, scale_in, sem_local, sem_amp, sem_data, sem_scale,
+):
+    panel, cap, obs = lax.axis_index("panel"), lax.axis_index("cap"), lax.axis_index("obs")
+    y, x = panel // 2, panel % 2
+    to_core = {"obs": 1 - obs}
+    to_y = {"panel": (1 - y) * 2 + x}
+    to_x = {"panel": y * 2 + 1 - x}
+    to_z = [{"cap": lax.rem(cap + d, CHIPS_Z)} for d in range(1, CHIPS_Z)]
+
+    barrier = pltpu.get_barrier_semaphore()
+    for target in [to_core, to_y, to_x] + to_z:
+        pl.semaphore_signal(barrier, inc=1, device_id=target, device_id_type=MESH)
+
+    half = 2 * BLK
+    own_half = amp_hbm.at[:, pl.ds(pl.multiple_of(obs * half, half), half), :]
+    local = [
+        pltpu.make_async_copy(src, dst, sem_local.at[i])
+        for i, (src, dst) in enumerate((
+            (surf_hbm, surf_ref), (cap_hbm, cap_ref), (own_half, amp_own),
+            (shift_hbm, shift_ref), (high_hbm, high_ref), (low_hbm, low_ref),
+        ))
+    ]
+    for copy in local:
+        copy.start()
+    pl.semaphore_wait(barrier, 6)
+
+    def remote(src, dst, sems, number, target):
+        return pltpu.make_async_remote_copy(
+            src_ref=src, dst_ref=dst, send_sem=sems.at[0, number], recv_sem=sems.at[1, number],
+            device_id=target, device_id_type=MESH,
+        )
+
+    amp_copy = remote(
+        amp_hbm.at[:, pl.ds(pl.multiple_of((1 - obs) * half, half), half), :], amp_in, sem_amp, 0, to_core)
+    amp_copy.start()
+
+    local[0].wait()
+    for tile in range(2):
+        rows = slice(tile * BLK, (tile + 1) * BLK)
+        for term in range(2):
+            v = surf_ref[term, rows, :]
+            after = jnp.concatenate([v[:, 1:], v[:, -1:]], axis=1)
+            before = jnp.concatenate([v[:, :1], v[:, :-1]], axis=1)
+            rate = after - before
+            for b in range(v.shape[1] // BLK):
+                series[tile, b, term * BLK:(term + 1) * BLK, :] = rate[:, b * BLK:(b + 1) * BLK]
+                if term == 1:
+                    series[tile, b, 2 * BLK:3 * BLK, :] = v[:, b * BLK:(b + 1) * BLK]
+
+    for copy in local[1:]:
+        copy.wait()
+    weight = jnp.where(cap_ref[...] >= CAPS, 1.0, 1.0 / CAPS).astype(jnp.float32)
+
+    def fill(side, amps):
+        for tile in range(2):
+            w = weight[:, tile * BLK:(tile + 1) * BLK]
+            for part in range(2):
+                for term in range(3):
+                    block = amps[term, tile * BLK:(tile + 1) * BLK, part * BLK:(part + 1) * BLK]
+                    lhs[side * 2 + part, tile, :, term * BLK:(term + 1) * BLK] = (
+                        block.astype(jnp.float32).T * (w * (1.0 if term == 2 else 0.5))
+                    ).astype(jnp.bfloat16)
+
+    def product(side, chunk):
+        largest = jnp.zeros((1, 1), jnp.float32)
+        for part in range(2):
+            column = (obs if side == 0 else 1 - obs) * 2 + part
+            total = jnp.zeros((BLK, CHUNK), jnp.float32)
+            for tile in range(2):
+                begin = KMAX - shift_ref[obs * 2 + tile, column] + chunk * (CHUNK // BLK)
+                window = jnp.concatenate([series[tile, begin + b] for b in range(CHUNK // BLK)], axis=1)
+                total += jnp.dot(lhs[side * 2 + part, tile], window, preferred_element_type=jnp.float32)
+            if side == 0:
+                acc[part * BLK:(part + 1) * BLK, chunk * CHUNK:(chunk + 1) * CHUNK] = total
+            else:
+                other[part * BLK:(part + 1) * BLK, :] = total
+                largest = jnp.maximum(largest, biggest(total))
+        return largest
+
+    sent = []
+
+    def send(number, scale, src, dst, target):
+        scale_out[number] = jnp.broadcast_to(scale, (8, 128))
+        pair = (
+            remote(scale_out.at[number], scale_in.at[number], sem_scale, number, target),
+            remote(src, dst, sem_data, number, target),
+        )
+        for copy in pair:
+            copy.start()
+            sent.append(copy)
+        return pair
+
+    def arrived(pair):
+        for copy in pair:
+            copy.wait_recv()
+
+    def take(number):
+        return scale_in[number][0:1, 0:1]
+
+    quarter = BLK // 2
+    rows = quarter // CHIPS_Z
+    coming = {}
+
+    def at(row, size):
+        return pl.ds(pl.multiple_of(row, rows), size)
+
+    def span(chunk):
+        return slice(chunk * CHUNK, (chunk + 1) * CHUNK)
+
+    def to_other_core(chunk):
+        scale = scale_of(product(1, chunk))
+        send_c[chunk] = code(other[...], scale)
+        coming["core", chunk] = send(6 * chunk, scale, send_c.at[chunk], recv_c.at[chunk], to_core)
+
+    def first(chunk):
+        arrived(coming["core", chunk])
+        acc[:, span(chunk)] += decode(recv_c[chunk], take(6 * chunk))
+        if chunk % 2 == 0:
+            give = acc[at((1 - y) * BLK, BLK), span(chunk)]
+        else:
+            give = jnp.concatenate([
+                acc[at((1 - x) * quarter, quarter), span(chunk)],
+                acc[at(BLK + (1 - x) * quarter, quarter), span(chunk)],
+            ], axis=0)
+        scale = scale_of(biggest(give))
+        send_a[chunk] = code(give, scale)
+        coming["first", chunk] = send(
+            6 * chunk + 1, scale, send_a.at[chunk], recv_a.at[chunk], to_y if chunk % 2 == 0 else to_x)
+
+    def second(chunk):
+        arrived(coming["first", chunk])
+        scale = take(6 * chunk + 1)
+        if chunk % 2 == 0:
+            acc[at(y * BLK, BLK), span(chunk)] += decode(recv_a[chunk], scale)
+            give = acc[at(y * BLK + (1 - x) * quarter, quarter), span(chunk)]
+        else:
+            for part in range(2):
+                acc[at(part * BLK + x * quarter, quarter), span(chunk)] += decode(
+                    recv_a[chunk, part * quarter:(part + 1) * quarter], scale)
+            give = acc[at((1 - y) * BLK + x * quarter, quarter), span(chunk)]
+        scale = scale_of(biggest(give))
+        send_b[chunk] = code(give, scale)
+        coming["second", chunk] = send(
+            6 * chunk + 2, scale, send_b.at[chunk], recv_b.at[chunk], to_x if chunk % 2 == 0 else to_y)
+
+    mine = y * BLK + x * quarter
+
+    def third(chunk):
+        arrived(coming["second", chunk])
+        acc[at(mine, quarter), span(chunk)] += decode(recv_b[chunk], take(6 * chunk + 2))
+        whole = acc[at(mine, quarter), span(chunk)]
+        scale = scale_of(biggest(whole))
+        send_z[chunk] = code(whole, scale)
+        for d in range(1, CHIPS_Z):
+            place = lax.rem(cap + d, CHIPS_Z) * rows
+            coming["third", chunk, d] = send(
+                6 * chunk + 2 + d, scale, send_z.at[chunk, at(place, rows)], recv_z.at[chunk, d - 1], to_z[d - 1])
+
+    def last(chunk):
+        signal = acc[at(mine + cap * rows, rows), span(chunk)]
+        for d in range(1, CHIPS_Z):
+            arrived(coming["third", chunk, d])
+            signal += decode(recv_z[chunk, d - 1], take(6 * chunk + 2 + d))
+        return signal
+
+    fill(0, amp_own)
+    amp_copy.wait()
+    fill(1, amp_in)
+    chunks = NT // CHUNK
+    to_other_core(0)
+    for chunk in range(chunks):
+        if chunk + 1 < chunks:
+            to_other_core(chunk + 1)
+        product(0, chunk)
+        first(chunk)
+    for stage in (second, third):
+        for chunk in range(chunks):
+            stage(chunk)
+    signal = jnp.concatenate([last(chunk) for chunk in range(chunks)], axis=1)
+
+    pieces = jnp.concatenate([signal[:, j * HOP:j * HOP + SEG] for j in range(NSEG)], axis=0)
+    top = pieces.astype(jnp.bfloat16)
+    rest = (pieces - top.astype(jnp.float32)).astype(jnp.bfloat16)
+    dot = functools.partial(jnp.dot, preferred_element_type=jnp.float32)
+    spectrum = dot(top, high_ref[...]) + (dot(rest, high_ref[...]) + dot(top, low_ref[...]))
+    power = spectrum[:, :NBIN] ** 2 + spectrum[:, NBIN:] ** 2
+    total = power[0:rows]
+    for j in range(1, NSEG):
+        total += power[j * rows:(j + 1) * rows]
+    out_ref[...] = total * (1.0 / norm)
+
+    for copy in sent:
+        copy.wait_send()
+
+
+def fused_shards(surface, cap_of, shift, amplitude):
+    high, low, norm = dft_tables()
+    rows = BLK // 8
+    chunks = NT // CHUNK
+    caps = cap_of.reshape(1, -1)
+    tables = jnp.asarray(high), jnp.asarray(low)
+    pair = [
+        pltpu.VMEM((chunks, size, CHUNK), jnp.int16)
+        for size in (2 * BLK, 2 * BLK, BLK, BLK, BLK // 2, BLK // 2, BLK // 2)
+    ]
+    out = pl.pallas_call(
+        functools.partial(fused, norm),
+        out_shape=jax.ShapeDtypeStruct((rows, NBIN), jnp.float32),
+        in_specs=[pl.BlockSpec(memory_space=pltpu.HBM)] * 6,
+        out_specs=pl.BlockSpec(memory_space=pltpu.VMEM),
+        scratch_shapes=[
+            pltpu.SMEM(shift.shape, jnp.int32),
+            pltpu.VMEM(surface.shape, surface.dtype),
+            pltpu.VMEM(caps.shape, jnp.int32),
+            pltpu.VMEM((3, 2 * BLK, 2 * BLK), jnp.bfloat16),
+            pltpu.VMEM(high.shape, jnp.bfloat16),
+            pltpu.VMEM(low.shape, jnp.bfloat16),
+            pltpu.VMEM((3, 2 * BLK, 2 * BLK), jnp.bfloat16),
+            pltpu.VMEM((2, surface.shape[2] // BLK, 3 * BLK, BLK), jnp.bfloat16),
+            pltpu.VMEM((4, 2, BLK, 3 * BLK), jnp.bfloat16),
+            pltpu.VMEM((2 * BLK, NT), jnp.float32),
+            pltpu.VMEM((2 * BLK, CHUNK), jnp.float32),
+            *pair,
+            pltpu.VMEM((chunks, CHIPS_Z - 1, rows, CHUNK), jnp.int16),
+            pltpu.VMEM((6 * chunks, 8, 128), jnp.float32),
+            pltpu.VMEM((6 * chunks, 8, 128), jnp.float32),
+            pltpu.SemaphoreType.DMA((6,)),
+            pltpu.SemaphoreType.DMA((2, 1)),
+            pltpu.SemaphoreType.DMA((2, 6 * chunks)),
+            pltpu.SemaphoreType.DMA((2, 6 * chunks)),
+        ],
+        compiler_params=pltpu.CompilerParams(
+            collective_id=0, has_side_effects=True, vmem_limit_bytes=63 * 1024 * 1024
+        ),
+    )(shift, surface, caps, amplitude, *tables)
+    return out[None]
+
+
+def suits(mesh):
+    return mesh.shape["panel"] == 4 and mesh.shape["cap"] == 4 and mesh.shape["obs"] == 2
+
+
 def solution(mesh):
     return jax.shard_map(
-        shards,
+        fused_shards if suits(mesh) else shards,
         mesh=mesh,
         in_specs=(
             P(None, ("panel", "cap", "obs"), None),

time: 187 us -> 32.5 us (0.17)
  waiting for transfers between devices: 104 us -> 0 us
  local copies, waits for them, and re-layouts: 41 us -> 1.32 us
  Pallas kernels: 0 us -> 30.9 us
  matrix products: 19 us -> 0 us
  between operations: 13.6 us -> 0.01 us
  other arithmetic: 9.47 us -> 0 us
    reduce_scatter x1 -> x0, waiting for transfers between devices: 82.9 us -> none  [reduce_rows(): lax.psum_scatter(partial_value, ('panel', 'cap'), scatter_dimension=1, ti...]
    pallas_call x0 -> x1, Pallas kernels: none -> 30.9 us  [fused_shards(): pl.pallas_call(functools.partial(fused, norm), out_shape=jax.ShapeDtypeSt...]
    gather x24 -> x0, local copies, waits for them, and re-layouts: 24.4 us -> none
    all_gather x1 -> x0, waiting for transfers between devices: 20.6 us -> none  [shards(): whole = lax.all_gather(local_series, 'obs', axis=1, tiled=True)]
    dot_general x5 -> x0, matrix products: 19 us -> none  [the longest x4 18.3 us: step(): jnp.einsum('cbqo,qcbn->qon', block, windows, preferred_element_type=jnp.f...]
    squeeze x4 -> x0, local copies, waits for them, and re-layouts: 6.69 us -> none  [partial_signal(): total = lax.scan(step, start, (tiles, delays, blocks))[0]]
    slice x4 -> x0, local copies, waits for them, and re-layouts: 5.79 us -> none  [the longest x2 4.62 us: make_series(): before = jnp.concatenate([values[:, :, :1], values[:, :, :-1]], axis=2)]
    convert_element_type x1 -> x0, other arithmetic: 3.06 us -> none  [make_series(): return stacked.astype(jnp.bfloat16)]
  transfers between devices with their start and end apart: 2 -> 0, of which waited for: 2 -> 0; matrix products, arithmetic and copies ran while one was open for 2% -> 0% of each run, Pallas kernels for 0% -> 0%
where the time goes in v2:
time: 32.5 us; the launch traced here: 32.3 us
  Pallas kernels  30.9 us (95%)
  local copies, waits for them, and re-layouts  1.32 us (4%)
    pallas_call x1, Pallas kernels, fused_shards(): pl.pallas_call(functools.partial(fused, norm), out_shape=jax.ShapeDtypeSt...  30.9 us
    unnamed x1, local copies, waits for them, and re-layouts  1.32 us

profile of v2, /device:TPU:0, one launch (start us, length us, event | category | flops | bytes accessed | tf_op | source)
XLA Modules:
  0.0 32.3 jit_solution(3820194115109811474)
XLA Ops:
  0.0 30.9 %shard_map.64 = f32[16,256]{1,0:T(8,128)} custom-call(s32[4,4]{1,0:T(4,128)} %shift_hbm.1, bf16[2,256,2560]{2,1,0:T(8,128)(2,1)} %surf_hbm.1, s32[1,256]{1,0:T(1,128)} %bitcast.3, bf16[3,512,256]{2,1,0:T(8,128)(2,1)} %amp_hbm.1, bf16[512,512]{1,0:T(8,128)(2,1)} %constant.4.clone.high_hbm, bf16[512,512]{1,0:T(8,128)(2,1)} %constant.5.clone.low_hbm), custom_call_target="tpu_custom_call" | custom-call | tf_op jit(solution)/shard_map/pallas_call | solution.py:332
  30.9 1.3 %copy.8 = f32[1,16,256]{2,1,0:T(8,128)} copy(f32[1,16,256]{2,1,0:T(8,128)} %bitcast.2) | data formatting | bytes 32768
